TPU v7x, 32 devices: a whole 2x2x4 slice. The times are simulated.
32 devices in a mesh: groups: 2 (over y), row: 2 (over x), col: 4 (over z), depth: 2 (over core).
Axes of the slice: x: 2, y: 2, z: 4, core: 2. Of those that a mesh axis runs over, the one named last changes fastest.
Arguments:
- layer_input: bfloat16 [4, 224, 4096], P(('groups', 'depth'), 'row', 'col'), parts along dimension 0, may hold values from -6 to 6
- out_grad: bfloat16 [4, 224, 4096], P(('groups', 'depth'), 'row', 'col'), parts along dimension 0, may hold values from -6 to 6
- gate_pre: bfloat16 [4, 224, 14336], P(('groups', 'depth'), 'col', 'row'), parts along dimension 0, may hold values from -6 to 6
- up_pre: bfloat16 [4, 224, 14336], P(('groups', 'depth'), 'col', 'row'), parts along dimension 0, may hold values from -6 to 6
- gate_weight: bfloat16 [4096, 14336], P('col', ('row', 'depth')), may hold values from -0.09375 to 0.09375
- up_weight: bfloat16 [4096, 14336], P('col', ('row', 'depth')), may hold values from -0.09375 to 0.09375
- down_weight: bfloat16 [14336, 4096], P(('row', 'depth'), 'col'), may hold values from -0.046875 to 0.046875
Outputs:
- input_grad: bfloat16 [4, 224, 4096], P(('groups', 'depth'), 'row', 'col'), parts along dimension 0
- gate_weight_grad: bfloat16 [4, 4096, 14336], P(('groups', 'depth'), 'col', 'row'), parts along dimension 0
- up_weight_grad: bfloat16 [4, 4096, 14336], P(('groups', 'depth'), 'col', 'row'), parts along dimension 0
- down_weight_grad: bfloat16 [4, 14336, 4096], P(('groups', 'depth'), 'row', 'col'), parts along dimension 0
There are 2 independent parts, one for each index of `groups`. A program takes and returns all parts, laid end to end along the dimension named above; an argument that names none is the same for every part. Nothing has to cross between parts.
All inputs are finite; a program needn't handle non-finite values.
Results may differ from a plain program's by a relative error of at most 0.03.
Values may be sent and summed in bfloat16 or wider, within the bound.
A program may use at most 192 MiB of HBM per device.

v0:
```python
import jax
import jax.numpy as jnp
from jax import lax
from jax.sharding import PartitionSpec as P


def swiglu_grads(hidden_grad, gate_rows, up_rows):
    gate_value = gate_rows.astype(jnp.float32)
    up_value = up_rows.astype(jnp.float32)
    sig = jax.nn.sigmoid(gate_value)
    silu_value = gate_value * sig
    hidden = (silu_value * up_value).astype(jnp.bfloat16)
    gate_grad = (hidden_grad * up_value * sig * (1.0 + gate_value * (1.0 - sig))).astype(
        jnp.bfloat16
    )
    up_grad = (hidden_grad * silu_value).astype(jnp.bfloat16)
    return (gate_grad, up_grad, hidden)


def times_transposed(left, right):
    return lax.dot_general(
        left, right, (((1,), (1,)), ((), ())), preferred_element_type=jnp.float32
    )


def over_tokens(left, right):
    return lax.dot_general(
        left, right, (((0,), (0,)), ((), ())), preferred_element_type=jnp.float32
    )


def shards(layer_input, out_grad, gate_pre, up_pre, gate_weight, up_weight, down_weight):
    gate_full, up_full, down_full = (
        lax.all_gather(gate_weight, "depth", axis=1, tiled=True),
        lax.all_gather(up_weight, "depth", axis=1, tiled=True),
        lax.all_gather(down_weight, "depth", axis=0, tiled=True),
    )
    input_rows, grad_rows = (
        lax.all_gather(layer_input[0], "row", axis=0, tiled=True),
        lax.all_gather(out_grad[0], "row", axis=0, tiled=True),
    )
    gate_rows, up_rows = (
        lax.all_gather(gate_pre[0], "col", axis=0, tiled=True),
        lax.all_gather(up_pre[0], "col", axis=0, tiled=True),
    )
    partial_hidden = times_transposed(grad_rows, down_full)
    hidden_grad = lax.psum(partial_hidden.astype(jnp.bfloat16), "col").astype(jnp.float32)
    gate_grad, up_grad, hidden = swiglu_grads(hidden_grad, gate_rows, up_rows)
    gate_wgrad = over_tokens(input_rows, gate_grad).astype(jnp.bfloat16)
    up_wgrad = over_tokens(input_rows, up_grad).astype(jnp.bfloat16)
    down_wgrad = over_tokens(hidden, grad_rows).astype(jnp.bfloat16)
    input_share = lax.psum_scatter(
        (times_transposed(gate_grad, gate_full) + times_transposed(up_grad, up_full)).astype(
            jnp.bfloat16
        ),
        "row",
        scatter_dimension=0,
        tiled=True,
    )
    return (input_share[None], gate_wgrad[None], up_wgrad[None], down_wgrad[None])


def solution(mesh):
    return jax.shard_map(
        shards,
        mesh=mesh,
        in_specs=(
            P(("groups", "depth"), "row", "col"),
            P(("groups", "depth"), "row", "col"),
            P(("groups", "depth"), "col", "row"),
            P(("groups", "depth"), "col", "row"),
            P("col", ("row", "depth")),
            P("col", ("row", "depth")),
            P(("row", "depth"), "col"),
        ),
        out_specs=(
            P(("groups", "depth"), "row", "col"),
            P(("groups", "depth"), "col", "row"),
            P(("groups", "depth"), "col", "row"),
            P(("groups", "depth"), "row", "col"),
        ),
        check_vma=False,
    )
```

profile of v0, /device:TPU:0, one launch (start us, length us, event | category | flops | bytes accessed | tf_op | source)
XLA Modules:
  0.0 433.5 jit_solution(16787232423276558372)
XLA Ops:
  7.2 0.0 copy-start.1
  7.2 0.0 all-gather.10.cloned.1.call-start
  7.2 0.7 all-gather.10.cloned.1.call-update
  7.9 0.0 all-gather.18.cloned.1.call-start
  8.0 0.7 all-gather.18.cloned.1.call-update
  8.7 0.0 all-gather.16.cloned.1.call-start
  8.7 0.7 all-gather.16.cloned.1.call-update
  9.4 0.0 all-reduce.2.cloned.1.call-start
  9.4 0.0 copy-done.1
  9.4 9.2 %all-gather = bf16[1,224,1024]{2,1,0:T(8,128)(2,1)S(1)} all-gather(bf16[1,112,1024]{2,1,0:T(8,128)(2,1)S(1)} %copy-done.1), channel_id=2, replica_groups=mesh['groups'=2,'row'=2,'col'=4,'depth'=2] {'row'}, dimensions={1}, use_global_device_ids=true | all-gather | bytes 688128 | tf_op jit(solution)/shard_map/all_gather | solution.py:40
  18.7 20.7 %all-gather.10.cloned.1.call-done = bf16[7168,1024]{1,0:T(8,128)(2,1)} async-done(((bf16[3584,1024]{1,0:T(8,128)(2,1)}), bf16[7168,1024]{1,0:T(8,128)(2,1)}) %all-gather.10.cloned.1.call-update) | async-done | bytes 14680080 | tf_op jit(solution)/shard_map/all_gather | solution.py:36
  39.3 15.9 %convolution_convert_fusion = bf16[224,7168]{1,0:T(8,128)(2,1)} fusion(bf16[7168,1024]{1,0:T(8,128)(2,1)} %all-gather.10.cloned.1.call-done, bf16[1,224,1024]{2,1,0:T(8,128)(2,1)S(1)} %all-gather), kind=kOutput, calls=%fused_computation.6 | convolution fusion | flops 3289939968 | bytes 18350080 | tf_op jit(solution)/shard_map/dot_general | solution.py:21
  55.3 0.0 all-reduce.2.cloned.1.call-update
  55.3 0.0 copy-start.2
  55.3 0.0 all-gather.12.cloned.1.call-start
  55.4 0.5 all-gather.12.cloned.1.call-update
  55.9 0.0 all-gather.14.cloned.1.call-start
  56.0 0.5 all-gather.14.cloned.1.call-update
  56.5 0.0 reduce-scatter.2.cloned.1.call-start
  56.5 0.0 copy-done.2
  56.5 8.7 %all-gather.3 = bf16[1,224,1024]{2,1,0:T(8,128)(2,1)} all-gather(bf16[1,112,1024]{2,1,0:T(8,128)(2,1)S(1)} %copy-done.2), channel_id=5, replica_groups=mesh['groups'=2,'row'=2,'col'=4,'depth'=2] {'row'}, dimensions={1}, use_global_device_ids=true | all-gather | bytes 688128 | tf_op jit(solution)/shard_map/all_gather | solution.py:39
  65.3 41.4 %all-gather.18.cloned.1.call-done = bf16[1,224,7168]{2,1,0:T(8,128)(2,1)} async-done(((bf16[1,56,7168]{2,1,0:T(8,128)(2,1)}), bf16[1,224,7168]{2,1,0:T(8,128)(2,1)}) %all-gather.18.cloned.1.call-update) | async-done | bytes 3211280 | tf_op jit(solution)/shard_map/all_gather | solution.py:43
  106.7 64.8 %all-gather.16.cloned.1.call-done = bf16[1,224,7168]{2,1,0:T(8,128)(2,1)} async-done(((bf16[1,56,7168]{2,1,0:T(8,128)(2,1)}), bf16[1,224,7168]{2,1,0:T(8,128)(2,1)}) %all-gather.16.cloned.1.call-update) | async-done | bytes 3211280 | tf_op jit(solution)/shard_map/all_gather | solution.py:44
  171.5 10.8 %convert_bitcast_fusion = bf16[1,7168,1024]{2,1,0:T(8,128)(2,1)} fusion(bf16[1,224,7168]{2,1,0:T(8,128)(2,1)} %all-gather.16.cloned.1.call-done, bf16[1,224,7168]{2,1,0:T(8,128)(2,1)} %all-gather.18.cloned.1.call-done, bf16[1,224,1024]{2,1,0:T(8,128)(2,1)S(1)} %all-gather), kind=kOutput, calls=%fused_computation | convolution fusion | flops 3308519424 | bytes 21561344 | tf_op jit(solution)/shard_map/dot_general | solution.py:27
  182.3 113.9 %all-reduce.2.cloned.1.call-done = bf16[224,7168]{1,0:T(8,128)(2,1)} async-done(((bf16[224,7168]{1,0:T(8,128)(2,1)}), bf16[224,7168]{1,0:T(8,128)(2,1)}) %all-reduce.2.cloned.1.call-update) | async-done | bytes 3211280 | tf_op jit(solution)/shard_map/psum | solution.py:47
  296.2 5.3 %fusion.3 = bf16[224,7168]{1,0:T(8,128)(2,1)S(1)} fusion(bf16[224,7168]{1,0:T(8,128)(2,1)} %all-reduce.2.cloned.1.call-done, bf16[1,224,7168]{2,1,0:T(8,128)(2,1)} %all-gather.16.cloned.1.call-done, bf16[1,224,7168]{2,1,0:T(8,128)(2,1)} %all-gather.18.cloned.1.call-done), kind=kLoop, calls=%fused_computation.13 | loop fusion | flops 20873216 | bytes 12845056 | tf_op jit(solution)/shard_map/convert_element_type | solution.py:13
  301.6 22.2 %all-gather.12.cloned.1.call-done = bf16[1024,7168]{1,0:T(8,128)(2,1)} async-done(((bf16[1024,3584]{1,0:T(8,128)(2,1)}), bf16[1024,7168]{1,0:T(8,128)(2,1)}) %all-gather.12.cloned.1.call-update) | async-done | bytes 14680080 | tf_op jit(solution)/shard_map/all_gather | solution.py:34
  323.8 8.7 %fusion.19 = f32[224,1024]{1,0:T(8,128)} fusion(bf16[224,7168]{1,0:T(8,128)(2,1)S(1)} %fusion.3, bf16[1024,7168]{1,0:T(8,128)(2,1)} %all-gather.12.cloned.1.call-done), kind=kOutput, calls=%fused_computation.27 | convolution fusion | flops 3288334336 | bytes 18808832 | tf_op jit(solution)/shard_map/dot_general | solution.py:21
  332.4 21.1 %all-gather.14.cloned.1.call-done = bf16[1024,7168]{1,0:T(8,128)(2,1)} async-done(((bf16[1024,3584]{1,0:T(8,128)(2,1)}), bf16[1024,7168]{1,0:T(8,128)(2,1)}) %all-gather.14.cloned.1.call-update) | async-done | bytes 14680080 | tf_op jit(solution)/shard_map/all_gather | solution.py:35
  353.5 12.8 %fusion.11 = bf16[224,1024]{1,0:T(8,128)(2,1)} fusion(f32[224,1024]{1,0:T(8,128)} %fusion.19, bf16[1024,7168]{1,0:T(8,128)(2,1)} %all-gather.14.cloned.1.call-done, bf16[224,7168]{1,0:T(8,128)(2,1)} %all-reduce.2.cloned.1.call-done, bf16[1,224,7168]{2,1,0:T(8,128)(2,1)} %all-gather.18.cloned.1.call-done), kind=kOutput, calls=%fused_computation.21 | convolution fusion | flops 3301638144 | bytes 22478848 | tf_op jit(solution)/shard_map/dot_general | solution.py:21
  366.3 0.0 reduce-scatter.2.cloned.1.call-update
  366.3 8.6 %convert_bitcast_fusion.2 = bf16[1,1024,7168]{1,2,0:T(8,128)(2,1)} fusion(bf16[224,7168]{1,0:T(8,128)(2,1)S(1)} %fusion.3, bf16[1,224,1024]{2,1,0:T(8,128)(2,1)} %all-gather.3), kind=kOutput, calls=%fused_computation.2 | convolution fusion | flops 3295674368 | bytes 18350080 | tf_op jit(solution)/shard_map/dot_general | solution.py:27
  374.9 0.0 copy-start
  374.9 20.1 %copy.11 = bf16[1,1024,7168]{2,1,0:T(8,128)(2,1)} copy(bf16[1,1024,7168]{1,2,0:T(8,128)(2,1)} %convert_bitcast_fusion.2) | data formatting | bytes 29360128
  395.0 0.0 copy-done
  395.0 11.7 %convert_bitcast_fusion.1 = bf16[1,1024,7168]{1,2,0:T(8,128)(2,1)} fusion(bf16[1,224,1024]{2,1,0:T(8,128)(2,1)} %all-gather.3, bf16[224,7168]{1,0:T(8,128)(2,1)} %all-reduce.2.cloned.1.call-done, bf16[1,224,7168]{2,1,0:T(8,128)(2,1)S(1)} %copy-done), kind=kOutput, calls=%fused_computation.1 | convolution fusion | flops 3308519424 | bytes 21561344 | tf_op jit(solution)/shard_map/dot_general | solution.py:27
  406.7 19.9 %copy.12 = bf16[1,1024,7168]{2,1,0:T(8,128)(2,1)} copy(bf16[1,1024,7168]{1,2,0:T(8,128)(2,1)} %convert_bitcast_fusion.1) | data formatting | bytes 29360128
  426.6 0.0 reduce-scatter.2.cloned.1.call-done
Async XLA Ops:
  7.2 2.3 copy-start.1
  7.2 32.2 %all-gather.10.cloned.1.call-start = ((), (), s32[]{:S(2)}) async-start(), calls=%async_computation.1 | async-start | bytes 22020096 | tf_op jit(solution)/shard_map/all_gather | solution.py:36
  7.9 98.8 %all-gather.18.cloned.1.call-start = ((), (), s32[]{:S(2)}) async-start(), calls=%async_computation.7 | async-start | bytes 4014080 | tf_op jit(solution)/shard_map/all_gather | solution.py:43
  8.7 162.9 %all-gather.16.cloned.1.call-start = ((), (), s32[]{:S(2)}) async-start(), calls=%async_computation.6 | async-start | bytes 4014080 | tf_op jit(solution)/shard_map/all_gather | solution.py:44
  9.4 286.8 %all-reduce.2.cloned.1.call-start = ((), (), s32[]{:S(2)}) async-start(), calls=%async_computation.2 | async-start | bytes 6422528 | tf_op jit(solution)/shard_map/psum | solution.py:47
  55.3 1.2 copy-start.2
  55.3 268.4 %all-gather.12.cloned.1.call-start = ((), (), s32[]{:S(2)}) async-start(), calls=%async_computation.3 | async-start | bytes 22020096 | tf_op jit(solution)/shard_map/all_gather | solution.py:34
  55.9 297.6 %all-gather.14.cloned.1.call-start = ((), (), s32[]{:S(2)}) async-start(), calls=%async_computation.4 | async-start | bytes 22020096 | tf_op jit(solution)/shard_map/all_gather | solution.py:35
  56.5 370.1 %reduce-scatter.2.cloned.1.call-start = ((), (), s32[]{:S(2)}) async-start(), calls=%async_computation.5 | async-start | bytes 688128 | tf_op jit(solution)/shard_map/reduce_scatter | solution.py:52
  374.9 20.1 %copy-start = (bf16[1,224,7168]{2,1,0:T(8,128)(2,1)S(1)}, bf16[1,224,7168]{2,1,0:T(8,128)(2,1)}, u32[]{:S(2)}) copy-start(bf16[1,224,7168]{2,1,0:T(8,128)(2,1)} %all-gather.18.cloned.1.call-done) | copy-start | bytes 9633796
Sparse Core Ops, SparseCore 0:
  9.6 29.7 all-gather.9
  40.9 65.7 all-gather.17
  108.3 63.2 all-gather.15
  174.3 121.8 all-reduce.1
  297.7 26.0 all-gather.11
  325.3 28.1 all-gather.13
  366.4 14.9 reduce-scatter.1
where the time goes:
time: 435 us; the launch traced here: 433 us
  waiting for transfers between devices  287 us (66%)
  matrix products  68.5 us (16%)
  local copies, waits for them, and re-layouts  40 us (9%)
  blocking collectives  17.9 us (4%)
  between operations  14.2 us (3%)
  other arithmetic  5.33 us (1%)
    psum x1, waiting for transfers between devices, shards(): lax.psum(partial_hidden.astype(jnp.bfloat16), 'col').astype(jnp.float32)  114 us
    all_gather x1, waiting for transfers between devices, shards(): lax.all_gather(up_pre[0], 'col', axis=0, tiled=True)  64.8 us
    all_gather x1, waiting for transfers between devices, shards(): lax.all_gather(gate_pre[0], 'col', axis=0, tiled=True)  41.4 us
    unnamed x8, local copies, waits for them, and re-layouts  40 us
    dot_general x3, matrix products, times_transposed(): lax.dot_general(left, right, (((1,), (1,)), ((), ())), preferred_element_...  37.4 us
    dot_general x3, matrix products, over_tokens(): lax.dot_general(left, right, (((0,), (0,)), ((), ())), preferred_element_...  31.2 us
    all_gather x1, waiting for transfers between devices, shards(): lax.all_gather(gate_weight, 'depth', axis=1, tiled=True)  22.2 us
    all_gather x1, waiting for transfers between devices, shards(): lax.all_gather(up_weight, 'depth', axis=1, tiled=True)  21.1 us
  transfers between devices with their start and end apart: 7, of which 6 were waited for; matrix products, arithmetic and copies ran while one was open for 23% of the time, Pallas kernels for 0%

commit v1 on v0

v1 whole, which is shorter than its diff:
```python
import functools

import jax
import jax.numpy as jnp
from jax import lax
from jax.experimental import pallas as pl
from jax.experimental.pallas import tpu as pltpu
from jax.sharding import PartitionSpec as P

MESH = pl.DeviceIdType.MESH
BF16 = jnp.bfloat16
F32 = jnp.float32


def dot_last(left, right):
    return lax.dot_general(
        left, right, (((1,), (1,)), ((), ())), preferred_element_type=F32
    )


def dot_first(left, right):
    return lax.dot_general(
        left, right, (((0,), (0,)), ((), ())), preferred_element_type=F32
    )


def exchange_kernel(
    n_row, n_col, n_chunk,
    x_in, og_in, g_in, u_in, gw_in, uw_in, dw_in,
    x_out, og_out, act_out, ig_out,
    og, gu, own, fin, bin_, fout, bout, res, acc, part, inbox, gw, uw, dw,
    og_send, og_recv, x_send, x_recv, dep_send, dep_recv, loc,
    gu_send, gu_recv, ar_send, ar_recv, res_send, res_recv, res_loc,
    ig_send, ig_recv, w_sem, dw_sem,
):
    row, col, dep = lax.axis_index("row"), lax.axis_index("col"), lax.axis_index("depth")
    other = 1 - dep
    toks = x_in.shape[1]
    small = g_in.shape[1]
    units = gw_in.shape[1]
    width = units // n_chunk
    me = dep * n_row + row
    n_peer = 2 * n_row
    has_next = col < n_col - 1
    has_prev = col > 0

    def peer(k):
        idx = lax.rem(me + k, n_peer)
        return idx, {"row": lax.rem(idx, n_row), "depth": idx // n_row}

    def next_prev(direction):
        if direction == 0:
            return has_prev, has_next, {"col": jnp.minimum(col + 1, n_col - 1)}
        return has_next, has_prev, {"col": jnp.maximum(col - 1, 0)}

    barrier = pltpu.get_barrier_semaphore()
    for k in range(1, n_peer):
        pl.semaphore_signal(barrier, inc=1, device_id=peer(k)[1], device_id_type=MESH)
    for direction in range(2):
        _, going, to = next_prev(direction)

        @pl.when(going)
        def _():
            pl.semaphore_signal(barrier, inc=1, device_id=to, device_id_type=MESH)

    load_gw = pltpu.make_async_copy(gw_in, gw, w_sem.at[0])
    load_uw = pltpu.make_async_copy(uw_in, uw, w_sem.at[1])

    def load_dw(i):
        slot = lax.rem(i, 2)
        return pltpu.make_async_copy(
            dw_in.at[pl.ds(i * width, width)], dw.at[slot], dw_sem.at[slot]
        )

    load_dw(0).start()
    own_g = [
        pltpu.make_async_copy(
            src.at[0, :, pl.ds(pl.multiple_of(dep * units, 128), units)],
            gu.at[a, col, dep], loc.at[a],
        )
        for a, src in enumerate((g_in, u_in))
    ]
    for copy in own_g:
        copy.start()
    own_og = pltpu.make_async_copy(og_in.at[0], og.at[me], loc.at[2])
    own_og.start()
    own_x = pltpu.make_async_copy(x_in.at[0], x_out.at[row], loc.at[3])
    own_x.start()

    beside = jnp.where(has_next, 1, 0) + jnp.where(has_prev, 1, 0)
    pl.semaphore_wait(barrier, n_peer - 1 + beside)

    dep_copies = [
        pltpu.make_async_remote_copy(
            src_ref=src.at[0, :, pl.ds(pl.multiple_of(other * units, 128), units)],
            dst_ref=gu.at[a, col, dep],
            send_sem=dep_send.at[a], recv_sem=dep_recv.at[a],
            device_id={"depth": other}, device_id_type=MESH,
        )
        for a, src in enumerate((g_in, u_in))
    ]

    def arrived(a):
        return pltpu.make_async_remote_copy(
            src_ref=gu.at[a, col, other], dst_ref=gu.at[a, col, other],
            send_sem=dep_send.at[a], recv_sem=dep_recv.at[a],
            device_id={"depth": other}, device_id_type=MESH,
        )

    def og_copy(k):
        idx, to = peer(k)
        return pltpu.make_async_remote_copy(
            src_ref=og_in.at[0], dst_ref=og.at[me],
            send_sem=og_send.at[k], recv_sem=og_recv.at[me],
            device_id=to, device_id_type=MESH,
        )

    def og_from(k):
        idx, to = peer(k)
        return pltpu.make_async_remote_copy(
            src_ref=og.at[idx], dst_ref=og.at[idx],
            send_sem=og_send.at[k], recv_sem=og_recv.at[idx],
            device_id=to, device_id_type=MESH,
        )

    def x_copy(k):
        idx = lax.rem(row + k, n_row)
        return pltpu.make_async_remote_copy(
            src_ref=x_in.at[0], dst_ref=x_out.at[row],
            send_sem=x_send.at[k], recv_sem=x_recv.at[row],
            device_id={"row": idx}, device_id_type=MESH,
        )

    def x_from(k):
        idx = lax.rem(row + k, n_row)
        return pltpu.make_async_remote_copy(
            src_ref=x_out.at[idx], dst_ref=x_out.at[idx],
            send_sem=x_send.at[k], recv_sem=x_recv.at[idx],
            device_id={"row": idx}, device_id_type=MESH,
        )

    def gu_copy(direction, block, a, s):
        to = next_prev(direction)[2]
        m = 2 * a + s
        return pltpu.make_async_remote_copy(
            src_ref=gu.at[a, block, s], dst_ref=gu.at[a, block, s],
            send_sem=gu_send.at[direction, block, m],
            recv_sem=gu_recv.at[direction, block, m],
            device_id=to, device_id_type=MESH,
        )

    for copy in dep_copies:
        copy.start()
    for k in range(1, n_peer):
        og_copy(k).start()
    for copy in own_g:
        copy.wait()
    for a in range(2):
        for direction in range(2):
            @pl.when(next_prev(direction)[1])
            def _():
                gu_copy(direction, col, a, dep).start()
    for a in range(2):
        arrived(a).wait_recv()
        for direction in range(2):
            @pl.when(next_prev(direction)[1])
            def _():
                gu_copy(direction, col, a, other).start()
    for k in range(1, n_row):
        x_copy(k).start()
    load_gw.start()
    load_uw.start()

    own_og.wait()
    for k in range(1, n_peer):
        og_from(k).wait_recv()
    keep_og = pltpu.make_async_copy(og.at[pl.ds(dep * n_row, n_row)], og_out, loc.at[4])
    keep_og.start()

    def partial(i, _):
        load_dw(i).wait()

        @pl.when(i + 1 < n_chunk)
        def _():
            load_dw(i + 1).start()
        rows = og[...].reshape(n_peer * toks, og.shape[2])
        product = dot_last(rows, dw[lax.rem(i, 2)])
        own[i] = product.reshape(2 * n_col, small, width).astype(BF16)
        return 0

    lax.fori_loop(0, n_chunk, partial, 0)

    def gu_step(step):
        for m in range(4):
            a, s = m % 2, m // 2
            for direction in range(2):
                coming, going, _ = next_prev(direction)
                block = col - 1 - step if direction == 0 else col + 1 + step
                valid = (block >= 0) & (block < n_col)
                half = dep if s == 0 else other

                @pl.when(valid)
                def _():
                    gu_copy(direction, block, a, half).wait_recv()

                    @pl.when(going)
                    def _():
                        gu_copy(direction, block, a, half).start()

    def gu_sent(step):
        for m in range(4):
            for direction in range(2):
                _, going, _ = next_prev(direction)
                block = col - step if direction == 0 else col + step
                valid = (block >= 0) & (block < n_col)

                @pl.when(valid & going)
                def _():
                    gu_copy(direction, block, m // 2, m % 2).wait_send()

    def ar_copy(direction, i, src):
        dst = fin if direction == 0 else bin_
        return pltpu.make_async_remote_copy(
            src_ref=src.at[i], dst_ref=dst.at[i],
            send_sem=ar_send.at[direction, i], recv_sem=ar_recv.at[direction, i],
            device_id=next_prev(direction)[2], device_id_type=MESH,
        )

    gu_step(0)
    gu_sent(0)
    for direction in range(2):
        coming, going, _ = next_prev(direction)

        @pl.when(jnp.logical_not(coming))
        def _():
            def first(i, _):
                ar_copy(direction, i, own).start()
                return 0
            lax.fori_loop(0, n_chunk, first, 0)
            land = fin if direction == 0 else bin_

            def clear(i, _):
                land[i] = jnp.zeros(land.shape[1:], BF16)
                return 0
            lax.fori_loop(0, n_chunk, clear, 0)

    if n_col > 2:
        def later(step, _):
            gu_step(step)
            return 0
        lax.fori_loop(1, n_col - 1, later, 0)

    load_gw.wait()
    load_uw.wait()
    acc[...] = jnp.zeros_like(acc)
    half_col = n_col // 2

    def res_copy(i):
        at = pl.multiple_of(dep * units + i * width, 128)
        return pltpu.make_async_remote_copy(
            src_ref=res.at[i, other], dst_ref=act_out.at[:, :, pl.ds(at, width)],
            send_sem=res_send.at[i], recv_sem=res_recv.at[i],
            device_id={"depth": other}, device_id_type=MESH,
        )

    def res_from(i):
        at = pl.multiple_of(other * units + i * width, 128)
        there = act_out.at[:, :, pl.ds(at, width)]
        return pltpu.make_async_remote_copy(
            src_ref=there, dst_ref=there,
            send_sem=res_send.at[i], recv_sem=res_recv.at[i],
            device_id={"depth": other}, device_id_type=MESH,
        )

    def res_keep(i):
        at = pl.multiple_of(dep * units + i * width, 128)
        return pltpu.make_async_copy(
            res.at[i, dep], act_out.at[:, :, pl.ds(at, width)], res_loc.at[i]
        )

    def slot(t, _):
        for direction in range(2):
            coming, going, _ = next_prev(direction)
            hops = col if direction == 0 else n_col - 1 - col
            i = t - hops
            land, leave = ((fin, fout), (bin_, bout))[direction]

            @pl.when(coming & (i >= 0) & (i < n_chunk))
            def _():
                ar_copy(direction, i, leave).wait_recv()

                @pl.when(going)
                def _():
                    leave[i] = (land[i].astype(F32) + own[i].astype(F32)).astype(BF16)
                    ar_copy(direction, i, leave).start()

        i = t - jnp.maximum(col, n_col - 1 - col)

        @pl.when((i >= 0) & (i < n_chunk))
        def _():
            cols = pl.ds(pl.multiple_of(i * width, 128), width)
            for s in range(2):
                def pair(p, _):
                    blocks = pl.ds(s * n_col + 2 * p, 2)
                    pair_at = pl.ds(2 * p, 2)
                    shape = (2 * small, width)
                    hg = (
                        fin[i, blocks].astype(F32) + own[i, blocks].astype(F32)
                        + bin_[i, blocks].astype(F32)
                    ).reshape(shape)
                    gate = gu[0, pair_at, s, :, cols].astype(F32).reshape(shape)
                    up = gu[1, pair_at, s, :, cols].astype(F32).reshape(shape)
                    sig = 1.0 / (1.0 + jnp.exp(-gate))
                    silu = gate * sig
                    at = pl.ds(pl.multiple_of(p * 2 * small, 16), 2 * small)
                    res[i, s, 0, at] = (hg * up * sig * (1.0 + gate * (1.0 - sig))).astype(BF16)
                    res[i, s, 1, at] = (hg * silu).astype(BF16)
                    res[i, s, 2, at] = (silu * up).astype(BF16)
                    return 0
                lax.fori_loop(0, half_col, pair, 0)
            res_copy(i).start()
            res_keep(i).start()
            for s in range(2):
                acc[s] += dot_last(res[i, s, 0], gw[:, cols]) + dot_last(res[i, s, 1], uw[:, cols])
        return 0

    lax.fori_loop(0, n_chunk + n_col - 1, slot, 0)

    part[...] = acc[...].reshape(part.shape).astype(BF16)

    def ig_copy(k):
        idx, to = peer(k)
        return pltpu.make_async_remote_copy(
            src_ref=part.at[idx], dst_ref=inbox.at[me],
            send_sem=ig_send.at[k], recv_sem=ig_recv.at[me],
            device_id=to, device_id_type=MESH,
        )

    def ig_from(k):
        idx, to = peer(k)
        return pltpu.make_async_remote_copy(
            src_ref=part.at[idx], dst_ref=inbox.at[idx],
            send_sem=ig_send.at[k], recv_sem=ig_recv.at[idx],
            device_id=to, device_id_type=MESH,
        )

    for k in range(1, n_peer):
        ig_copy(k).start()

    def finish(i, _):
        res_from(i).wait_recv()
        res_copy(i).wait_send()
        res_keep(i).wait()
        for direction in range(2):
            @pl.when(next_prev(direction)[1])
            def _():
                ar_copy(direction, i, own).wait_send()
        return 0

    lax.fori_loop(0, n_chunk, finish, 0)
    if n_col > 1:
        def sent(step, _):
            gu_sent(step)
            return 0
        lax.fori_loop(1, n_col - 1, sent, 0)
    for copy in dep_copies:
        copy.wait_send()
    own_x.wait()
    keep_og.wait()
    for k in range(1, n_row):
        x_copy(k).wait_send()
        x_from(k).wait_recv()
    total = part[me].astype(F32)
    for k in range(1, n_peer):
        og_copy(k).wait_send()
        ig_from(k).wait_recv()
        total += inbox[peer(k)[0]].astype(F32)
    ig_out[0] = total.astype(BF16)
    for k in range(1, n_peer):
        ig_copy(k).wait_send()


def exchange(n_row, n_col, x, og, g, u, gw, uw, dw):
    toks, feats = x.shape[1:]
    small = g.shape[1]
    units = gw.shape[1]
    n_chunk = 14 if units % (14 * 128) == 0 else 7
    width = units // n_chunk
    n_peer = 2 * n_row
    subtok = toks * n_row
    anywhere = pl.BlockSpec(memory_space=pl.ANY)
    line = pltpu.VMEM((n_chunk, 2 * n_col, small, width), BF16)
    dma = pltpu.SemaphoreType.DMA
    return pl.pallas_call(
        functools.partial(exchange_kernel, n_row, n_col, n_chunk),
        out_shape=(
            jax.ShapeDtypeStruct((n_row, toks, feats), BF16),
            jax.ShapeDtypeStruct((n_row, toks, feats), BF16),
            jax.ShapeDtypeStruct((3, subtok, 2 * units), BF16),
            jax.ShapeDtypeStruct((1, toks, feats), BF16),
        ),
        in_specs=[anywhere] * 7,
        out_specs=(anywhere, anywhere, anywhere, pl.BlockSpec(memory_space=pltpu.VMEM)),
        scratch_shapes=[
            pltpu.VMEM((n_peer, toks, feats), BF16),
            pltpu.VMEM((2, n_col, 2, small, units), BF16),
            line, line, line, line, line,
            pltpu.VMEM((n_chunk, 2, 3, subtok, width), BF16),
            pltpu.VMEM((2, subtok, feats), F32),
            pltpu.VMEM((n_peer, toks, feats), BF16),
            pltpu.VMEM((n_peer, toks, feats), BF16),
            pltpu.VMEM((feats, units), BF16),
            pltpu.VMEM((feats, units), BF16),
            pltpu.VMEM((2, width, feats), BF16),
            dma((n_peer,)), dma((n_peer,)), dma((n_row,)), dma((n_row,)),
            dma((2,)), dma((2,)), dma((5,)),
            dma((2, n_col, 4)), dma((2, n_col, 4)),
            dma((2, n_chunk)), dma((2, n_chunk)),
            dma((n_chunk,)), dma((n_chunk,)), dma((n_chunk,)),
            dma((n_peer,)), dma((n_peer,)), dma((2,)), dma((2,)),
        ],
        compiler_params=pltpu.CompilerParams(
            collective_id=0, has_side_effects=True, vmem_limit_bytes=63 * 2**20
        ),
        name="exchange",
    )(x, og, g, u, gw, uw, dw)


def weight_grad_kernel(x_ref, og_ref, act_ref, gate_ref, up_ref, down_ref):
    x = x_ref[...]
    gate_ref[0] = dot_first(x, act_ref[0]).astype(BF16)
    up_ref[0] = dot_first(x, act_ref[1]).astype(BF16)
    down_ref[0] = dot_first(act_ref[2], og_ref[...]).astype(BF16)


def weight_grads(x, og, act):
    subtok, feats = x.shape
    units = act.shape[2]
    tile = 512 if units % 512 == 0 else 256
    whole = pl.BlockSpec((subtok, feats), lambda i: (0, 0))
    wide = pl.BlockSpec((1, feats, tile), lambda i: (0, 0, i))
    return pl.pallas_call(
        weight_grad_kernel,
        grid=(units // tile,),
        out_shape=(
            jax.ShapeDtypeStruct((1, feats, units), BF16),
            jax.ShapeDtypeStruct((1, feats, units), BF16),
            jax.ShapeDtypeStruct((1, units, feats), BF16),
        ),
        in_specs=[whole, whole, pl.BlockSpec((3, subtok, tile), lambda i: (0, 0, i))],
        out_specs=(wide, wide, pl.BlockSpec((1, tile, feats), lambda i: (0, i, 0))),
        compiler_params=pltpu.CompilerParams(vmem_limit_bytes=40 * 2**20),
        name="weight_grads",
    )(x, og, act)


def solution(mesh):
    n_row, n_col = mesh.shape["row"], mesh.shape["col"]

    def shards(x, og, g, u, gw, uw, dw):
        x_all, og_all, act, ig = exchange(n_row, n_col, x, og, g, u, gw, uw, dw)
        feats = x.shape[2]
        return (ig, *weight_grads(x_all.reshape(-1, feats), og_all.reshape(-1, feats), act))

    return jax.shard_map(
        shards,
        mesh=mesh,
        in_specs=(
            P(("groups", "depth"), "row", "col"),
            P(("groups", "depth"), "row", "col"),
            P(("groups", "depth"), "col", "row"),
            P(("groups", "depth"), "col", "row"),
            P("col", ("row", "depth")),
            P("col", ("row", "depth")),
            P(("row", "depth"), "col"),
        ),
        out_specs=(
            P(("groups", "depth"), "row", "col"),
            P(("groups", "depth"), "col", "row"),
            P(("groups", "depth"), "col", "row"),
            P(("groups", "depth"), "row", "col"),
        ),
        check_vma=False,
    )
```

time: 435 us -> 218 us (0.50)
  waiting for transfers between devices: 287 us -> 0 us
  Pallas kernels: 0 us -> 210 us
  matrix products: 68.5 us -> 0 us
  local copies, waits for them, and re-layouts: 40 us -> 6.46 us
  blocking collectives: 17.9 us -> 0 us
  between operations: 14.2 us -> 0.65 us
  other arithmetic: 5.33 us -> 0 us
    pallas_call x0 -> x2, Pallas kernels: none -> 210 us  [the longest x1 192 us: exchange(): pl.pallas_call(functools.partial(exchange_kernel, n_row, n_col, n_chunk),...]
    all_gather x5 -> x0, waiting for transfers between devices: 170 us -> none  [the longest x1 64.8 us: shards(): lax.all_gather(up_pre[0], 'col', axis=0, tiled=True)]
    psum x1 -> x0, waiting for transfers between devices: 114 us -> none  [shards(): lax.psum(partial_hidden.astype(jnp.bfloat16), 'col').astype(jnp.float32)]
    dot_general x6 -> x0, matrix products: 68.5 us -> none  [the longest x3 37.4 us: times_transposed(): lax.dot_general(left, right, (((1,), (1,)), ((), ())), preferred_element_...]
    unnamed x8 -> x9, local copies, waits for them, and re-layouts: 40 us -> 6.46 us
    all_gather x2 -> x0, blocking collectives: 17.9 us -> none  [the longest x1 9.2 us: shards(): lax.all_gather(out_grad[0], 'row', axis=0, tiled=True)]
    convert_element_type x1 -> x0, other arithmetic: 5.33 us -> none  [swiglu_grads(): (hidden_grad * up_value * sig * (1.0 + gate_value * (1.0 - sig))).astype(...]
  transfers between devices with their start and end apart: 7 -> 0, of which waited for: 6 -> 0; matrix products, arithmetic and copies ran while one was open for 23% -> 0% of each run, Pallas kernels for 0% -> 0%
where the time goes in v1:
time: 218 us; the launch traced here: 217 us
  Pallas kernels  210 us (96%)
  local copies, waits for them, and re-layouts  6.46 us (3%)
    pallas_call x1, Pallas kernels, exchange(): pl.pallas_call(functools.partial(exchange_kernel, n_row, n_col, n_chunk),...  192 us
    pallas_call x1, Pallas kernels, weight_grads(): pl.pallas_call(weight_grad_kernel, grid=(units // tile,), out_shape=(jax....  17.9 us
    unnamed x9, local copies, waits for them, and re-layouts  6.46 us

profile of v1, /device:TPU:0, one launch (start us, length us, event | category | flops | bytes accessed | tf_op | source)
XLA Modules:
  0.0 217.2 jit_solution(15320135970012427653)
XLA Ops:
  0.6 192.1 %exchange.1 = (bf16[2,112,1024]{2,1,0:T(8,128)(2,1)}, bf16[2,112,1024]{2,1,0:T(8,128)(2,1)}, bf16[3,224,7168]{2,1,0:T(8,128)(2,1)}, bf16[1,112,1024]{2,1,0:T(8,128)(2,1)}) custom-call(bf16[1,112,1024]{2,1,0:T(8,128)(2,1)} %x_in.1, bf16[1,112,1024]{2,1,0:T(8,128)(2,1)} %og_in.1, bf16[1,56,7168]{2,1,0:T(8,128)(2,1)} %g_in.1, bf16[1,56,7168]{2,1,0:T(8,128)(2,1)} %u_in.1, ...), custom_call_target="tpu_custom_call" | custom-call | tf_op jit(solution)/shard_map/exchange/pallas_call | solution.py:394
  192.8 0.0 copy-start
  192.8 3.7 %copy-done = bf16[3,224,7168]{2,1,0:T(8,128)(2,1)S(1)} copy-done((bf16[3,224,7168]{2,1,0:T(8,128)(2,1)S(1)}, bf16[3,224,7168]{2,1,0:T(8,128)(2,1)}, u32[]{:S(2)}) %copy-start) | copy-done | bytes 9633816
  196.5 0.0 copy-start.1
  196.5 1.0 copy-done.1
  197.5 0.0 copy-start.2
  197.5 1.0 copy-done.2
  198.6 0.0 copy-start.3
  198.6 17.9 %weight_grads.1 = (bf16[1,1024,7168]{2,1,0:T(8,128)(2,1)}, bf16[1,1024,7168]{2,1,0:T(8,128)(2,1)}, bf16[1,7168,1024]{2,1,0:T(8,128)(2,1)}) custom-call(bf16[224,1024]{1,0:T(8,128)(2,1)S(1)} %bitcast.2, bf16[224,1024]{1,0:T(8,128)(2,1)S(1)} %bitcast.3, bf16[3,224,7168]{2,1,0:T(8,128)(2,1)S(1)} %copy-done), custom_call_target="tpu_custom_call" | custom-call | tf_op jit(solution)/shard_map/weight_grads/pallas_call | solution.py:442
  216.5 0.0 copy-done.3
  216.5 0.7 copy.12
Async XLA Ops:
  192.8 3.7 %copy-start = (bf16[3,224,7168]{2,1,0:T(8,128)(2,1)S(1)}, bf16[3,224,7168]{2,1,0:T(8,128)(2,1)}, u32[]{:S(2)}) copy-start(bf16[3,224,7168]{2,1,0:T(8,128)(2,1)} %get-tuple-element.14.act_ref) | copy-start | bytes 28901380
  196.5 1.0 copy-start.1
  197.5 1.0 copy-start.2
  198.6 17.9 %copy-start.3 = (bf16[1,112,1024]{2,1,0:T(8,128)(2,1)S(1)}, bf16[1,112,1024]{2,1,0:T(8,128)(2,1)}, u32[]{:S(2)}) copy-start(bf16[1,112,1024]{2,1,0:T(8,128)(2,1)} %get-tuple-element.22) | copy-start | bytes 688132

commit v2 on v1

--- a/solution.py
+++ b/solution.py
@@ -27,12 +27,15 @@
 def exchange_kernel(
     n_row, n_col, n_chunk,
     x_in, og_in, g_in, u_in, gw_in, uw_in, dw_in,
-    x_out, og_out, act_out, ig_out,
-    og, gu, own, fin, bin_, fout, bout, res, acc, part, inbox, gw, uw, dw,
-    og_send, og_recv, x_send, x_recv, dep_send, dep_recv, loc,
-    gu_send, gu_recv, ar_send, ar_recv, res_send, res_recv, res_loc,
-    ig_send, ig_recv, w_sem, dw_sem,
+    x_out, og_out, act_out, *rest,
 ):
+    shares = rest[: 2 * n_row]
+    (
+        og, gu, own, fin, bin_, fout, bout, res, acc, gw, uw, dw,
+        og_send, og_recv, x_send, x_recv, dep_send, dep_recv, loc,
+        gu_send, gu_recv, ar_send, ar_recv, res_send, res_recv, res_loc,
+        w_sem, dw_sem,
+    ) = rest[2 * n_row :]
     row, col, dep = lax.axis_index("row"), lax.axis_index("col"), lax.axis_index("depth")
     other = 1 - dep
     toks = x_in.shape[1]
@@ -321,31 +324,16 @@
             res_copy(i).start()
             res_keep(i).start()
             for s in range(2):
-                acc[s] += dot_last(res[i, s, 0], gw[:, cols]) + dot_last(res[i, s, 1], uw[:, cols])
+                of_sub = pl.ds(s * n_row, n_row)
+                acc[of_sub] += (
+                    dot_last(res[i, s, 0], gw[:, cols]) + dot_last(res[i, s, 1], uw[:, cols])
+                ).reshape(n_row, toks, acc.shape[2])
         return 0
 
     lax.fori_loop(0, n_chunk + n_col - 1, slot, 0)
 
-    part[...] = acc[...].reshape(part.shape).astype(BF16)
-
-    def ig_copy(k):
-        idx, to = peer(k)
-        return pltpu.make_async_remote_copy(
-            src_ref=part.at[idx], dst_ref=inbox.at[me],
-            send_sem=ig_send.at[k], recv_sem=ig_recv.at[me],
-            device_id=to, device_id_type=MESH,
-        )
-
-    def ig_from(k):
-        idx, to = peer(k)
-        return pltpu.make_async_remote_copy(
-            src_ref=part.at[idx], dst_ref=inbox.at[idx],
-            send_sem=ig_send.at[k], recv_sem=ig_recv.at[idx],
-            device_id=to, device_id_type=MESH,
-        )
-
-    for k in range(1, n_peer):
-        ig_copy(k).start()
+    for k in range(n_peer):
+        shares[k][...] = acc[peer(k)[0]].astype(BF16)
 
     def finish(i, _):
         res_from(i).wait_recv()
@@ -370,14 +358,8 @@
     for k in range(1, n_row):
         x_copy(k).wait_send()
         x_from(k).wait_recv()
-    total = part[me].astype(F32)
     for k in range(1, n_peer):
         og_copy(k).wait_send()
-        ig_from(k).wait_recv()
-        total += inbox[peer(k)[0]].astype(F32)
-    ig_out[0] = total.astype(BF16)
-    for k in range(1, n_peer):
-        ig_copy(k).wait_send()
 
 
 def exchange(n_row, n_col, x, og, g, u, gw, uw, dw):
@@ -397,18 +379,16 @@
             jax.ShapeDtypeStruct((n_row, toks, feats), BF16),
             jax.ShapeDtypeStruct((n_row, toks, feats), BF16),
             jax.ShapeDtypeStruct((3, subtok, 2 * units), BF16),
-            jax.ShapeDtypeStruct((1, toks, feats), BF16),
+            *[jax.ShapeDtypeStruct((toks, feats), BF16)] * n_peer,
         ),
         in_specs=[anywhere] * 7,
-        out_specs=(anywhere, anywhere, anywhere, pl.BlockSpec(memory_space=pltpu.VMEM)),
+        out_specs=(anywhere, anywhere, anywhere, *[pl.BlockSpec(memory_space=pltpu.VMEM)] * n_peer),
         scratch_shapes=[
             pltpu.VMEM((n_peer, toks, feats), BF16),
             pltpu.VMEM((2, n_col, 2, small, units), BF16),
             line, line, line, line, line,
             pltpu.VMEM((n_chunk, 2, 3, subtok, width), BF16),
-            pltpu.VMEM((2, subtok, feats), F32),
-            pltpu.VMEM((n_peer, toks, feats), BF16),
-            pltpu.VMEM((n_peer, toks, feats), BF16),
+            pltpu.VMEM((n_peer, toks, feats), F32),
             pltpu.VMEM((feats, units), BF16),
             pltpu.VMEM((feats, units), BF16),
             pltpu.VMEM((2, width, feats), BF16),
@@ -417,7 +397,7 @@
             dma((2, n_col, 4)), dma((2, n_col, 4)),
             dma((2, n_chunk)), dma((2, n_chunk)),
             dma((n_chunk,)), dma((n_chunk,)), dma((n_chunk,)),
-            dma((n_peer,)), dma((n_peer,)), dma((2,)), dma((2,)),
+            dma((2,)), dma((2,)),
         ],
         compiler_params=pltpu.CompilerParams(
             collective_id=0, has_side_effects=True, vmem_limit_bytes=63 * 2**20
@@ -449,7 +429,12 @@
         ),
         in_specs=[whole, whole, pl.BlockSpec((3, subtok, tile), lambda i: (0, 0, i))],
         out_specs=(wide, wide, pl.BlockSpec((1, tile, feats), lambda i: (0, i, 0))),
-        compiler_params=pltpu.CompilerParams(vmem_limit_bytes=40 * 2**20),
+        compiler_params=pltpu.CompilerParams(vmem_limit_bytes=60 * 2**20),
+        cost_estimate=pl.CostEstimate(
+            flops=6 * subtok * feats * units,
+            bytes_accessed=6 * units * (feats + subtok) + 4 * subtok * feats,
+            transcendentals=0,
+        ),
         name="weight_grads",
     )(x, og, act)
 
@@ -457,10 +442,21 @@
 def solution(mesh):
     n_row, n_col = mesh.shape["row"], mesh.shape["col"]
 
+    def at(i):
+        return i % n_row * 2 + i // n_row
+
     def shards(x, og, g, u, gw, uw, dw):
-        x_all, og_all, act, ig = exchange(n_row, n_col, x, og, g, u, gw, uw, dw)
-        feats = x.shape[2]
-        return (ig, *weight_grads(x_all.reshape(-1, feats), og_all.reshape(-1, feats), act))
+        x_all, og_all, act, *parts = exchange(n_row, n_col, x, og, g, u, gw, uw, dw)
+        feats, n_peer = x.shape[2], 2 * n_row
+        arrived = [
+            lax.ppermute(
+                parts[k], ("row", "depth"), [(at(i), at((i + k) % n_peer)) for i in range(n_peer)]
+            )
+            for k in range(1, n_peer)
+        ]
+        grads = weight_grads(x_all.reshape(-1, feats), og_all.reshape(-1, feats), act)
+        total = sum((part.astype(F32) for part in arrived), parts[0].astype(F32))
+        return (total.astype(BF16)[None], *grads)
 
     return jax.shard_map(
         shards,

time: 218 us -> 207 us (0.950)
  Pallas kernels: 210 us -> 203 us
  local copies, waits for them, and re-layouts: 6.46 us -> 0.01 us
    pallas_call x1, Pallas kernels: 192 us -> 182 us  [exchange(): pl.pallas_call(functools.partial(exchange_kernel, n_row, n_col, n_chunk),...]
    unnamed x9 -> x2, local copies, waits for them, and re-layouts: 6.46 us -> 0.01 us
    pallas_call x1, Pallas kernels: 17.9 us -> 20.7 us  [weight_grads(): pl.pallas_call(weight_grad_kernel, grid=(units // tile,), out_shape=(jax....]
  transfers between devices with their start and end apart: 0 -> 3, of which waited for: 0 -> 0; matrix products, arithmetic and copies ran while one was open for 0% -> 0% of each run, Pallas kernels for 0% -> 10%
where the time goes in v2:
time: 207 us; the launch traced here: 206 us
  Pallas kernels  203 us (98%)
  starting transfers between devices  2.17 us (1%)
    pallas_call x1, Pallas kernels, exchange(): pl.pallas_call(functools.partial(exchange_kernel, n_row, n_col, n_chunk),...  182 us
    pallas_call x1, Pallas kernels, weight_grads(): pl.pallas_call(weight_grad_kernel, grid=(units // tile,), out_shape=(jax....  20.7 us
  transfers between devices with their start and end apart: 3, of which 0 were waited for; matrix products, arithmetic and copies ran while one was open for 0% of the time, Pallas kernels for 10%

profile of v2, /device:TPU:0, one launch (start us, length us, event | category | flops | bytes accessed | tf_op | source)
XLA Modules:
  0.0 206.3 jit_solution(14282566735345530406)
XLA Ops:
  0.6 182.0 %exchange.1 = (bf16[2,112,1024]{2,1,0:T(8,128)(2,1)}, bf16[2,112,1024]{2,1,0:T(8,128)(2,1)}, bf16[3,224,7168]{2,1,0:T(8,128)(2,1)}, bf16[112,1024]{1,0:T(8,128)(...) custom-call(bf16[1,112,1024]{2,1,0:T(8,128)(2,1)} %x_in.1, ...), custom_call_target="tpu_custom_call" | custom-call | tf_op jit(solution)/shard_map/exchange/pallas_call | solution.py:376
  182.6 1.1 collective-permute-start
  183.8 0.1 collective-permute-start.1
  183.8 1.0 collective-permute-start.2
  184.8 0.0 copy-start
  184.8 20.7 %weight_grads.1 = (bf16[1,1024,7168]{2,1,0:T(8,128)(2,1)}, bf16[1,1024,7168]{2,1,0:T(8,128)(2,1)}, bf16[1,7168,1024]{2,1,0:T(8,128)(2,1)}) custom-call(bf16[224,1024]{1,0:T(8,128)(2,1)} %bitcast.4, bf16[224,1024]{1,0:T(8,128)(2,1)} %bitcast.5, bf16[3,224,7168]{2,1,0:T(8,128)(2,1)} %get-tuple-element.20.act_ref), custom_call_target="tpu_custom_call" | custom-call | flops 9865003008 | bytes 54591488 | tf_op jit(solution)/shard_map/weight_grads/pallas_call | solution.py:422
  205.5 0.0 collective-permute-done
  205.5 0.0 collective-permute-done.1
  205.5 0.0 collective-permute-done.2
  205.5 0.0 copy-done
  205.5 0.8 fusion
Async XLA Ops:
  182.6 22.8 %collective-permute-start = (bf16[112,1024]{1,0:T(8,128)(2,1)}, bf16[112,1024]{1,0:T(8,128)(2,1)S(1)}, u32[]{:S(2)}, u32[]{:S(2)}) collective-permute-start(bf16[112,1024]{1,0:T(8,128)(2,1)} %get-tuple-element.15), channel_id=1, source_target_pairs={{0,8},{8,1},{1,9},{9,0},{2,10},{10,3},{3,11},{11,2},{4,12},{12,5},... | collective-permute-start | bytes 688136 | tf_op jit(solution)/shard_map/ppermute | solution.py:452
  183.8 21.7 %collective-permute-start.1 = (bf16[112,1024]{1,0:T(8,128)(2,1)}, bf16[112,1024]{1,0:T(8,128)(2,1)S(1)}, u32[]{:S(2)}, u32[]{:S(2)}) collective-permute-start(bf16[112,1024]{1,0:T(8,128)(2,1)} %get-tuple-element.16), channel_id=1, source_target_pairs={{0,1},{8,9},{1,0},{9,8},{2,3},{10,11},{3,2},{11,10},{4,5},{12,13},... | collective-permute-start | bytes 688136 | tf_op jit(solution)/shard_map/ppermute | solution.py:452
  183.8 21.6 %collective-permute-start.2 = (bf16[112,1024]{1,0:T(8,128)(2,1)}, bf16[112,1024]{1,0:T(8,128)(2,1)S(1)}, u32[]{:S(2)}, u32[]{:S(2)}) collective-permute-start(bf16[112,1024]{1,0:T(8,128)(2,1)} %get-tuple-element.17), channel_id=1, source_target_pairs={{0,9},{8,0},{1,8},{9,1},{2,11},{10,2},{3,10},{11,3},{4,13},{12,4},... | collective-permute-start | bytes 688136 | tf_op jit(solution)/shard_map/ppermute | solution.py:452
  184.8 20.7 %copy-start = (bf16[112,1024]{1,0:T(8,128)(2,1)S(1)}, bf16[112,1024]{1,0:T(8,128)(2,1)}, u32[]{:S(2)}) copy-start(bf16[112,1024]{1,0:T(8,128)(2,1)} %get-tuple-element.14) | copy-start | bytes 688132

commit v3 on v2

--- a/solution.py
+++ b/solution.py
@@ -152,10 +152,6 @@
             device_id=to, device_id_type=MESH,
         )
 
-    for copy in dep_copies:
-        copy.start()
-    for k in range(1, n_peer):
-        og_copy(k).start()
     for copy in own_g:
         copy.wait()
     for a in range(2):
@@ -163,6 +159,10 @@
             @pl.when(next_prev(direction)[1])
             def _():
                 gu_copy(direction, col, a, dep).start()
+    for copy in dep_copies:
+        copy.start()
+    for k in range(1, n_peer):
+        og_copy(k).start()
     for a in range(2):
         arrived(a).wait_recv()
         for direction in range(2):
@@ -302,7 +302,7 @@
         @pl.when((i >= 0) & (i < n_chunk))
         def _():
             cols = pl.ds(pl.multiple_of(i * width, 128), width)
-            for s in range(2):
+            for s in (other, dep):
                 def pair(p, _):
                     blocks = pl.ds(s * n_col + 2 * p, 2)
                     pair_at = pl.ds(2 * p, 2)
@@ -321,7 +321,8 @@
                     res[i, s, 2, at] = (silu * up).astype(BF16)
                     return 0
                 lax.fori_loop(0, half_col, pair, 0)
-            res_copy(i).start()
+                if s is other:
+                    res_copy(i).start()
             res_keep(i).start()
             for s in range(2):
                 of_sub = pl.ds(s * n_row, n_row)
@@ -416,7 +417,7 @@
 def weight_grads(x, og, act):
     subtok, feats = x.shape
     units = act.shape[2]
-    tile = 512 if units % 512 == 0 else 256
+    tile = max(t for t in range(128, 1025, 128) if units % t == 0)
     whole = pl.BlockSpec((subtok, feats), lambda i: (0, 0))
     wide = pl.BlockSpec((1, feats, tile), lambda i: (0, 0, i))
     return pl.pallas_call(

time: 207 us -> 205 us (level)
  Pallas kernels: 203 us -> 200 us
    pallas_call x1, Pallas kernels: 20.7 us -> 18.3 us  [weight_grads(): pl.pallas_call(weight_grad_kernel, grid=(units // tile,), out_shape=(jax....]
  transfers between devices with their start and end apart: 3 -> 3, of which waited for: 0 -> 0; matrix products, arithmetic and copies ran while one was open for 0% -> 0% of each run, Pallas kernels for 10% -> 9%
where the time goes in v3:
time: 205 us; the launch traced here: 204 us
  Pallas kernels  200 us (98%)
  starting transfers between devices  2.17 us (1%)
    pallas_call x1, Pallas kernels, exchange(): pl.pallas_call(functools.partial(exchange_kernel, n_row, n_col, n_chunk),...  182 us
    pallas_call x1, Pallas kernels, weight_grads(): pl.pallas_call(weight_grad_kernel, grid=(units // tile,), out_shape=(jax....  18.3 us
  transfers between devices with their start and end apart: 3, of which 0 were waited for; matrix products, arithmetic and copies ran while one was open for 0% of the time, Pallas kernels for 9%

profile of v3, /device:TPU:0, one launch (start us, length us, event | category | flops | bytes accessed | tf_op | source)
XLA Modules:
  0.0 203.8 jit_solution(14006247972034168582)
XLA Ops:
  0.6 181.8 %exchange.1 = (bf16[2,112,1024]{2,1,0:T(8,128)(2,1)}, bf16[2,112,1024]{2,1,0:T(8,128)(2,1)}, bf16[3,224,7168]{2,1,0:T(8,128)(2,1)}, bf16[112,1024]{1,0:T(8,128)(...) custom-call(bf16[1,112,1024]{2,1,0:T(8,128)(2,1)} %x_in.1, ...), custom_call_target="tpu_custom_call" | custom-call | tf_op jit(solution)/shard_map/exchange/pallas_call | solution.py:377
  182.4 1.1 collective-permute-start
  183.6 0.1 collective-permute-start.1
  183.7 1.0 collective-permute-start.2
  184.6 0.0 copy-start
  184.6 18.3 %weight_grads.1 = (bf16[1,1024,7168]{2,1,0:T(8,128)(2,1)}, bf16[1,1024,7168]{2,1,0:T(8,128)(2,1)}, bf16[1,7168,1024]{2,1,0:T(8,128)(2,1)}) custom-call(bf16[224,1024]{1,0:T(8,128)(2,1)} %bitcast.4, bf16[224,1024]{1,0:T(8,128)(2,1)} %bitcast.5, bf16[3,224,7168]{2,1,0:T(8,128)(2,1)} %get-tuple-element.20.act_ref), custom_call_target="tpu_custom_call" | custom-call | flops 9865003008 | bytes 54591488 | tf_op jit(solution)/shard_map/weight_grads/pallas_call | solution.py:423
  203.0 0.0 collective-permute-done
  203.0 0.0 collective-permute-done.1
  203.0 0.0 collective-permute-done.2
  203.0 0.0 copy-done
  203.0 0.8 fusion
Async XLA Ops:
  182.4 20.5 %collective-permute-start = (bf16[112,1024]{1,0:T(8,128)(2,1)}, bf16[112,1024]{1,0:T(8,128)(2,1)S(1)}, u32[]{:S(2)}, u32[]{:S(2)}) collective-permute-start(bf16[112,1024]{1,0:T(8,128)(2,1)} %get-tuple-element.15), channel_id=1, source_target_pairs={{0,8},{8,1},{1,9},{9,0},{2,10},{10,3},{3,11},{11,2},{4,12},{12,5},... | collective-permute-start | bytes 688136 | tf_op jit(solution)/shard_map/ppermute | solution.py:453
  183.6 19.4 %collective-permute-start.1 = (bf16[112,1024]{1,0:T(8,128)(2,1)}, bf16[112,1024]{1,0:T(8,128)(2,1)S(1)}, u32[]{:S(2)}, u32[]{:S(2)}) collective-permute-start(bf16[112,1024]{1,0:T(8,128)(2,1)} %get-tuple-element.16), channel_id=1, source_target_pairs={{0,1},{8,9},{1,0},{9,8},{2,3},{10,11},{3,2},{11,10},{4,5},{12,13},... | collective-permute-start | bytes 688136 | tf_op jit(solution)/shard_map/ppermute | solution.py:453
  183.7 19.3 %collective-permute-start.2 = (bf16[112,1024]{1,0:T(8,128)(2,1)}, bf16[112,1024]{1,0:T(8,128)(2,1)S(1)}, u32[]{:S(2)}, u32[]{:S(2)}) collective-permute-start(bf16[112,1024]{1,0:T(8,128)(2,1)} %get-tuple-element.17), channel_id=1, source_target_pairs={{0,9},{8,0},{1,8},{9,1},{2,11},{10,2},{3,10},{11,3},{4,13},{12,4},... | collective-permute-start | bytes 688136 | tf_op jit(solution)/shard_map/ppermute | solution.py:453
  184.6 18.4 %copy-start = (bf16[112,1024]{1,0:T(8,128)(2,1)S(1)}, bf16[112,1024]{1,0:T(8,128)(2,1)}, u32[]{:S(2)}) copy-start(bf16[112,1024]{1,0:T(8,128)(2,1)} %get-tuple-element.14) | copy-start | bytes 688132
